TPU v7x, 256 devices: a whole 4x4x8 slice. The times are simulated.
256 devices in a mesh: dp: 16 (over y, z_hi), tp: 16 (over x, z_lo, core).
Axes of the slice: x: 4, y: 4, z: 8 (z_hi: 4, z_lo: 2; z = z_hi * 2 + z_lo), core: 2. Of those that a mesh axis runs over, the one named last changes fastest.
Arguments:
- input_rows: bfloat16 [16, 2048, 4096], P('dp', 'tp'), may hold values from -6 to 6
- queries: bfloat16 [16, 2048, 4096], P('dp', None, 'tp')
- key_values: bfloat16 [16, 2048, 1024], P('dp')
- out_grad: bfloat16 [16, 2048, 4096], P('dp', None, 'tp'), may hold values from -6 to 6
- item_logratio: float32 [16, 4], P('dp'), may hold values from -40 to 40
- pair_ids: int32 [16, 4], P('dp'), may hold values from 0 to 1, as said below
- tile_item: int32 [16, 16], P('dp'), may hold values from 0 to 3, as said below
- tile_image: int32 [16, 16], P('dp'), may hold values from 0 to 16, as said below
Outputs:
- grad_query: bfloat16 [16, 2048, 4096], P('dp', None, 'tp')
- grad_kv_weight: float32 [4096, 1024], P('dp', 'tp')
Inputs may be any that keep to these rules, and one draw needn't show every extreme that they name: Each sequence's tile_item never falls, starts at 0 and ends at 3; a response may have no tiles. `tile_image`: image tiles carry 1 plus the index of the first tile of their image; an image is a maximal run of image tiles inside one response; the last tile of a sequence is an image tile and the one before it is text. `pair_ids`: within a sequence each pair id appears for exactly two responses; the earlier of the two is the chosen response.
All inputs are finite; a program needn't handle non-finite values.
Results may differ from a plain program's by a relative error of at most 0.0065.
Values may be sent and summed in bfloat16 or wider, within the bound.
A program may use at most 128 MiB of HBM per device.

v0:
```python
import functools, math
import jax, jax.numpy as jnp
from jax import lax
from jax.experimental import pallas as pl
from jax.experimental.pallas import tpu as pltpu

from jax.sharding import PartitionSpec as P

KVH = 4; HD = 128; TILE = 128; BETA = 0.1
MASKED = -1e30
LOG2E = 1.4426950408889634

def attention_kernel(ratio_h, pair_h, item_h, image_h, q_hbm, og_hbm, kv_hbm, dq_hbm, kvt_ref,
                     kv, q_ref, og_ref, dq_ref, s0, s1, dp0, dp1, acc, ratio, pair, item, image,
                     lo_s, hi_s, n_s, order, work, z_s, small_sem, big_sem, dq_sem):
    group = lax.axis_size("tp") // KVH
    g = lax.axis_index("tp") // group
    nt = item.shape[1]
    items = ratio.shape[1]
    small = [pltpu.make_async_copy(a, b, small_sem.at[i])
             for i, (a, b) in enumerate(((ratio_h, ratio), (pair_h, pair), (item_h, item), (image_h, image)))]
    for cp in small:
        cp.start()
    big = [pltpu.make_async_copy(kv_hbm.at[0, :, pl.ds(pl.multiple_of(g * 2 * HD, 2 * HD), 2 * HD)], kv, big_sem.at[0]),
           pltpu.make_async_copy(q_hbm.at[0], q_ref, big_sem.at[1]),
           pltpu.make_async_copy(og_hbm.at[0], og_ref, big_sem.at[2])]
    for cp in big:
        cp.start()
    inv_root = 1.0 / math.sqrt(HD)
    c2 = inv_root * LOG2E
    W = 2 * TILE
    acc[...] = jnp.zeros_like(acc)
    for cp in small:
        cp.wait()
    lo_s[0] = 0
    for i in range(1, nt):
        lo_s[i] = jnp.where(item[0, i] == item[0, i - 1], lo_s[i - 1], i)
    hi_s[nt - 1] = nt - 1
    for i in reversed(range(nt - 1)):
        same = (image[0, i] > 0) & (image[0, i] == image[0, i + 1]) & (item[0, i] == item[0, i + 1])
        hi_s[i] = jnp.where(same, hi_s[i + 1], i)
    for a in range(items):
        other = jnp.float32(0.0)
        p = jnp.float32(1.0)
        for b in range(items):
            if b != a:
                same = pair[0, a] == pair[0, b]
                other = other + jnp.where(same, ratio[0, b], 0.0)
                if a < b:
                    p = jnp.where(same, -1.0, p)
        z_s[a] = BETA * p * (other - ratio[0, a])
        z_s[items + a] = p

    for i in range(nt):
        n_s[i] = (hi_s[i] - lo_s[i] + 2) // 2

    def place(t, pos):
        i = lax.rem(t, nt)
        order[pos] = i
        return pos + jnp.where(n_s[i] == nt // 2 - t // nt, 1, 0)

    lax.fori_loop(0, nt * nt // 2, place, jnp.int32(0))

    def match(t, carry):
        i, w = carry
        a = order[jnp.minimum(i, nt - 1)]
        b = order[jnp.minimum(i + 1, nt - 1)]
        both = (i + 1 < nt) & (n_s[a] - n_s[b] <= 1)
        more = i < nt
        work[3 * w] = a
        work[3 * w + 1] = jnp.where(both, b, a)
        work[3 * w + 2] = jnp.where(both, 1, 0)
        return i + jnp.where(both, 2, 1), w + jnp.where(more, 1, 0)

    _, count = lax.fori_loop(0, nt, match, (jnp.int32(0), jnp.int32(0)))
    for cp in big:
        cp.wait()

    def block(I, real, n, spare, s_scr, dp_scr):
        lo = lo_s[I]
        hi = hi_s[I]
        img = image[0, I]
        it = item[0, I]
        r0 = pl.multiple_of(I * TILE, TILE)
        st = pl.multiple_of(jnp.clip(hi + 1 - 2 * n, 0, nt - 2 * n) * TILE, TILE)
        first = lo * TILE - st
        v = {}

        def stage1():
            qi = q_ref[pl.ds(r0, TILE), :]
            q2 = jnp.concatenate([qi[:, :HD], qi[:, HD:]], axis=0)
            coef = z_s[items + it] * real.astype(jnp.float32) / (1.0 + jnp.exp(jnp.full((8, HD), z_s[it], jnp.float32)))
            coef = jnp.concatenate([coef[:1], coef[:1]], axis=1)
            wi = (og_ref[pl.ds(r0, TILE), :].astype(jnp.float32) * coef).astype(jnp.bfloat16)
            w2 = jnp.concatenate([wi[:, :HD], wi[:, HD:]], axis=0)
            v["q2t"] = q2.T
            v["w2t"] = w2.T
            row = lax.broadcasted_iota(jnp.int32, (TILE, 1), 0)
            row = jnp.concatenate([row, row], axis=0)
            last = jnp.where(img > 0, jnp.full((2 * TILE, 1), (hi + 1) * TILE - 1 - st), r0 - st + row)
            m = None
            for ch in range(n):
                rows = pl.ds(st + ch * W, W)
                s = lax.dot_general(q2, kv[rows, :HD], (((1,), (1,)), ((), ())), preferred_element_type=jnp.float32)
                if ch <= spare or ch >= n - 2:
                    col = lax.broadcasted_iota(jnp.int32, (1, W), 1) + ch * W
                    ok = (col <= last) & (col >= first)
                    s = jnp.where(ok, s, MASKED)
                s_scr[:, ch * W:(ch + 1) * W] = s
                mm = jnp.maximum(s[:, :HD], s[:, HD:])
                m = mm if m is None else jnp.maximum(m, mm)
                dp_scr[:, ch * W:(ch + 1) * W] = lax.dot_general(
                    w2, kv[rows, HD:], (((1,), (1,)), ((), ())), preferred_element_type=jnp.float32)
            v["m"] = jnp.max(m, axis=1, keepdims=True) * c2

        def stage2():
            mr = v["m"]
            l = r = None
            for ch in range(n):
                cols = slice(ch * W, (ch + 1) * W)
                p = jnp.exp2(s_scr[:, cols] * c2 - mr)
                s_scr[:, cols] = p
                pd = p * dp_scr[:, cols]
                ll = p[:, :HD] + p[:, HD:]
                rr = pd[:, :HD] + pd[:, HD:]
                l = ll if l is None else l + ll
                r = rr if r is None else r + rr
            v["inv"] = 1.0 / jnp.sum(l, axis=1, keepdims=True)
            v["rd"] = jnp.sum(r, axis=1, keepdims=True) * v["inv"]

        def stage3():
            inv, rd = v["inv"], v["rd"]
            dq = None
            for ch in range(n):
                rows = pl.ds(st + ch * W, W)
                cols = slice(ch * W, (ch + 1) * W)
                at = s_scr[:, cols] * inv
                ds = (at * (dp_scr[:, cols] - rd)).astype(jnp.bfloat16)
                at = at.astype(jnp.bfloat16)
                d = jnp.dot(ds, kv[rows, :HD], preferred_element_type=jnp.float32)
                dq = d if dq is None else dq + d
                acc[:HD, rows] += jnp.dot(v["q2t"], ds, preferred_element_type=jnp.float32)
                acc[HD:, rows] += jnp.dot(v["w2t"], at, preferred_element_type=jnp.float32)
            dq = (dq * inv_root).astype(jnp.bfloat16)
            to = pl.ds(pl.multiple_of(jnp.where(real > 0, I, nt) * TILE, TILE), TILE)
            dq_ref[to, :HD] = dq[:TILE]
            dq_ref[to, HD:] = dq[TILE:]

        return stage1, stage2, stage3

    def out_copy(i):
        here = pl.ds(pl.multiple_of(i * TILE, TILE), TILE)
        return pltpu.make_async_copy(dq_ref.at[here], dq_hbm.at[0, here], dq_sem.at[i])

    def row_pair(j, carry):
        a, b, real = work[3 * j], work[3 * j + 1], work[3 * j + 2]
        n_here = n_s[a]
        for n in range(1, nt // 2 + 1):
            @pl.when(n_here == n)
            def _():
                one = block(a, jnp.int32(1), n, 1, s0, dp0)
                two = block(b, real, n, 1, s1, dp1)
                for f, g2 in zip(one, two):
                    f()
                    g2()
        out_copy(a).start()

        @pl.when(real > 0)
        def _():
            out_copy(b).start()
        return carry

    lax.fori_loop(0, count, row_pair, 0)
    for i in range(nt // 4):
        for z in range(2):
            frm = slice((2 * i + z) * W, (2 * i + z + 1) * W)
            to = slice(i * W, (i + 1) * W)
            kvt_ref[0, z, :, to] = (acc[:HD, frm] * inv_root).astype(jnp.bfloat16)
            kvt_ref[1, z, :, to] = acc[HD:, frm].astype(jnp.bfloat16)

    def finish(i, carry):
        out_copy(i).wait()
        return carry
    lax.fori_loop(0, nt, finish, 0)


def attention(queries, out_grad, key_values, ratio, pair, item, image):
    L = queries.shape[1]
    nt = L // TILE
    hbm = pl.BlockSpec(memory_space=pl.ANY)
    wide = pltpu.VMEM((2 * TILE, L), jnp.float32)
    low = pltpu.VMEM((L, 2 * HD), jnp.bfloat16)
    return pl.pallas_call(
        attention_kernel,
        out_shape=[jax.ShapeDtypeStruct(queries.shape, jnp.bfloat16),
                   jax.ShapeDtypeStruct((2, 2, HD, L // 2), jnp.bfloat16)],
        in_specs=[hbm] * 7,
        out_specs=[hbm, pl.BlockSpec(memory_space=pltpu.VMEM)],
        scratch_shapes=[low, low, low, pltpu.VMEM((L + TILE, 2 * HD), jnp.bfloat16), wide, wide, wide, wide,
            pltpu.VMEM((2 * HD, L), jnp.float32),
            pltpu.SMEM(ratio.shape, jnp.float32),
            pltpu.SMEM(pair.shape, jnp.int32),
            pltpu.SMEM(item.shape, jnp.int32),
            pltpu.SMEM(image.shape, jnp.int32),
            pltpu.SMEM((nt,), jnp.int32),
            pltpu.SMEM((nt,), jnp.int32),
            pltpu.SMEM((nt,), jnp.int32),
            pltpu.SMEM((nt + 1,), jnp.int32),
            pltpu.SMEM((3 * (nt + 1),), jnp.int32),
            pltpu.SMEM((2 * ratio.shape[1],), jnp.float32),
            pltpu.SemaphoreType.DMA((4,)), pltpu.SemaphoreType.DMA((3,)), pltpu.SemaphoreType.DMA((nt,)),
        ],
        compiler_params=pltpu.CompilerParams(vmem_limit_bytes=56 << 20),
        cost_estimate=pl.CostEstimate(flops=10 * 10**9, bytes_accessed=8 << 20, transcendentals=0),
        name="attention",
    )(ratio, pair, item, image, queries, out_grad, key_values)


CHUNKS = 4
PARTS = CHUNKS // 2
TIMES = ((0, 1), (1, 1), (2.2, 1), (3.3, 1), (5.4, 1), (6.5, 1))
SHARE = (0.5, 0.5, 0.5, 0.5)
MESH = pl.DeviceIdType.MESH
F32 = jnp.float32
BF16 = jnp.bfloat16


def exchange_kernel(kvt, x_own, x1, x2, x3, out_ref,
                    own, core_in, part, z_in, heads, xs, prod, y_out, y_in, final, turned, landed,
                    core_s, core_r, z_s, z_r, right_s, right_r, left_s, left_r,
                    fr_s, fr_r, fl_s, fl_r, y_s, y_r,
                    load_sem, x_sem, xs_s, xs_r, turn_s, turn_r, out_s, out_r):
    dp = lax.axis_index("dp")
    tp = lax.axis_index("tp")
    y = dp // 4
    zh = dp % 4
    x = tp // 4
    zl = tp // 2 % 2
    c = tp % 2
    rows, length = z_in.shape[1:]
    cols = xs.shape[3]
    half = length // 2
    sibling = (dp, x * 4 + zl * 2 + (1 - c))
    across = (dp, x * 4 + (1 - zl) * 2 + c)
    around = [(lax.rem(y + j, 4) * 4 + zh, tp) for j in range(4)]
    beside = [(dp, lax.rem(x + j, 4) * 4 + zl * 2 + c) for j in range(4)]
    right, left = beside[1], beside[3]

    load = pltpu.make_async_copy(kvt.at[c], own, load_sem)
    load.start()
    x_loads = []
    wide = cols // 4

    def piece(j, i):
        return x_own.at[:, pl.ds(pl.multiple_of((4 * i + lax.rem(x + j, 4)) * wide, wide), wide)]

    def place(i):
        return xs.at[x, c, :, pl.ds(i * wide, wide)]

    for i in range(4):
        cp = pltpu.make_async_copy(piece(0, i), place(i), x_sem.at[i])
        cp.start()
        x_loads.append(cp)
    xa = [None]
    for j, src in enumerate((x1, x2, x3)):
        cp = pltpu.make_async_copy(src, xs.at[lax.rem(x + 3 - j, 4), c], x_sem.at[4 + j])
        cp.start()
        xa.append([cp])

    barrier = pltpu.get_barrier_semaphore()
    for partner in (sibling, across, *beside[1:], *around[1:]):
        pl.semaphore_signal(barrier, 1, device_id=partner, device_id_type=MESH)

    def dest(u, h):
        return y * 4 + h, x * 4 + c * 2 + u

    def is_other(d, t):
        return jnp.logical_or(d != dp, t != tp)

    def greet(d, t, n):
        other = is_other(d, t)

        @pl.when(other)
        def _():
            pl.semaphore_signal(barrier, 1, device_id=(d, t), device_id_type=MESH)
        return n + jnp.where(other, 1, 0)

    n = lax.fori_loop(0, 8, lambda i, n: greet(*dest(i % 2, i // 2), n), jnp.int32(8))
    n = lax.fori_loop(0, 8, lambda i, n: greet(y * 4 + i // 2, x * 4 + i % 2 * 2 + zl, n), n)
    pl.semaphore_wait(barrier, n)

    started = []

    def send(src, dst, ss, rs, to):
        cp = pltpu.make_async_remote_copy(src_ref=src, dst_ref=dst, send_sem=ss, recv_sem=rs,
                                          device_id=to, device_id_type=MESH)
        cp.start()
        started.append(cp)
        return cp

    def cut(k):
        return pl.ds(k * rows, rows)

    core = [send(kvt.at[1 - c, :, cut(k)], core_in.at[k], core_s.at[k], core_r.at[k], sibling)
            for k in range(CHUNKS)]
    load.wait()

    zc, rc, lc, frc, flc, yc, tc, xc = ([] for _ in range(8))

    def share(j):
        for cp in xa[j] or x_loads:
            cp.wait()
        here = xs.at[lax.rem(x + 4 - j, 4), c]
        xc.append(send(here, here, xs_s.at[j], xs_r.at[j], sibling))

    def reduce_core(k):
        core[k].wait_recv()
        part[k] = (own[1 - zl, cut(k)].astype(F32) + core_in[k, 1 - zl].astype(F32)).astype(BF16)
        zc.append(send(part.at[k], z_in.at[k], z_s.at[k], z_r.at[k], across))

    def reduce_z(k):
        zc[k].wait_recv()
        heads[k, x] = (own[zl, cut(k)].astype(F32) + core_in[k, zl].astype(F32) + z_in[k].astype(F32)).astype(BF16)
        here = heads.at[k, x]
        rc.append(send(here, here, right_s.at[k], right_r.at[k], right))
        lc.append(send(here, here, left_s.at[k], left_r.at[k], left))

    def forward(k):
        rc[k].wait_recv()
        a = heads.at[k, lax.rem(x + 3, 4), :, pl.ds(0, half)]
        frc.append(send(a, a, fr_s.at[k], fr_r.at[k], right))
        lc[k].wait_recv()
        b = heads.at[k, lax.rem(x + 1, 4), :, pl.ds(half, half)]
        flc.append(send(b, b, fl_s.at[k], fl_r.at[k], left))

    def multiply(k):
        frc[k].wait_recv()
        flc[k].wait_recv()
        if k == 0:
            for cp in xc:
                cp.wait_recv()
        lhs = heads[k].reshape(4 * rows, length)
        res = jnp.dot(lhs, xs[...].reshape(length, cols), preferred_element_type=F32)
        for q in range(4):
            prod[k, q] = res[:, q * wide:(q + 1) * wide]
        sent = []
        for j in (2, 1, 3):
            y_out[k, j - 1] = prod[k, lax.rem(y + j, 4)].astype(BF16)
            sent.append(send(y_out.at[k, j - 1], y_in.at[k, j - 1], y_s.at[k, j - 1], y_r.at[k, j - 1], around[j]))
        yc.append(sent)

    spot = zh * 2 + zl

    def out_copy(k, q):
        d, t = dest(k // PARTS, lax.rem(x + 4 - q, 4))
        return d, t, pltpu.make_async_remote_copy(
            src_ref=turned.at[k, q], dst_ref=landed.at[spot, k % PARTS], send_sem=out_s.at[k * 4 + q],
            recv_sem=out_r.at[spot, k % PARTS], device_id=(d, t), device_id_type=MESH)

    def deliver(k):
        for cp in yc[k]:
            cp.wait_recv()
        total = (prod[k, y] + y_in[k, 0].astype(F32) + y_in[k, 1].astype(F32) + y_in[k, 2].astype(F32)).astype(BF16)
        for h in range(4):
            final[k, h] = total[h * rows:(h + 1) * rows]
        turned[k, 0] = final[k, x]
        tc.append([send(final.at[k, lax.rem(x + j, 4)], turned.at[k, j], turn_s.at[k, j - 1], turn_r.at[k, j - 1],
                        beside[j]) for j in (2, 1, 3)])

    def scatter(k):
        for cp in tc[k]:
            cp.wait_recv()

        def one(q, carry):
            d, t, cp = out_copy(k, q)
            other = is_other(d, t)

            @pl.when(other)
            def _():
                cp.start()

            @pl.when(jnp.logical_not(other))
            def _():
                pltpu.make_async_copy(turned.at[k, q], landed.at[spot, k % PARTS], out_r.at[spot, k % PARTS]).start()
            return carry
        lax.fori_loop(0, 4, one, 0)

    stages = (reduce_core, reduce_z, forward, multiply, deliver, scatter)
    order = sorted((start + k * gap, i, k) for i, (start, gap) in enumerate(TIMES) for k in range(CHUNKS))
    order = sorted(order + [(SHARE[j], -1, j) for j in range(4)])
    for _, i, k in order:
        share(k) if i < 0 else stages[i](k)

    def collect(i, total):
        new = []
        for p in range(PARTS):
            pltpu.make_async_copy(landed.at[i, p], landed.at[i, p], out_r.at[i, p]).wait()
            new.append(total[p] + landed[i, p].astype(F32))
        return tuple(new)

    zero = jnp.zeros((rows, cols // 4), F32)
    sums = lax.fori_loop(0, 8, collect, (zero,) * PARTS)
    for p in range(PARTS):
        out_ref[p * rows:(p + 1) * rows] = sums[p]

    for cp in started:
        cp.wait_send()

    def drain(j, carry):
        d, t, cp = out_copy(j // 4, j % 4)

        @pl.when(is_other(d, t))
        def _():
            cp.wait_send()
        return carry
    lax.fori_loop(0, 4 * CHUNKS, drain, 0)


def exchange(kvt, x_own, others):
    length = kvt.shape[3]
    cols = x_own.shape[1] // 4
    rows = HD // CHUNKS
    sem = pltpu.SemaphoreType.DMA
    n = CHUNKS
    return pl.pallas_call(
        exchange_kernel,
        out_shape=jax.ShapeDtypeStruct((PARTS * rows, cols // 4), F32),
        in_specs=[pl.BlockSpec(memory_space=pl.ANY)] * 5,
        out_specs=pl.BlockSpec(memory_space=pltpu.VMEM),
        scratch_shapes=[
            pltpu.VMEM((2, HD, length), BF16), pltpu.VMEM((n, 2, rows, length), BF16),
            pltpu.VMEM((n, rows, length), BF16), pltpu.VMEM((n, rows, length), BF16),
            pltpu.VMEM((n, 4, rows, length), BF16), pltpu.VMEM((4, 2, TILE, cols), BF16),
            pltpu.VMEM((n, 4, 4 * rows, cols // 4), F32),
            pltpu.VMEM((n, 3, 4 * rows, cols // 4), BF16), pltpu.VMEM((n, 3, 4 * rows, cols // 4), BF16),
            pltpu.VMEM((n, 4, rows, cols // 4), BF16), pltpu.VMEM((n, 4, rows, cols // 4), BF16),
            pltpu.VMEM((8, PARTS, rows, cols // 4), BF16),
        ] + [sem((n,))] * 12 + [sem((n, 3))] * 2 + [sem, sem((7,)), sem((4,)), sem((4,)),
                                                    sem((n, 3)), sem((n, 3)), sem((4 * n,)), sem((8, PARTS))],
        compiler_params=pltpu.CompilerParams(collective_id=0, has_side_effects=True, vmem_limit_bytes=56 << 20),
        cost_estimate=pl.CostEstimate(flops=10**9, bytes_accessed=8 << 20, transcendentals=0),
        name="exchange",
    )(kvt, x_own, *others)


def deal_kernel(x_in, *rest):
    outs, sem = rest[:3], rest[3]
    x = lax.axis_index("tp") // 4
    wide = outs[0].shape[1] // 4
    copies = []
    for j in range(1, 4):
        for i in range(4):
            src = x_in.at[:, pl.ds(pl.multiple_of((4 * i + lax.rem(x + j, 4)) * wide, wide), wide)]
            copies.append(pltpu.make_async_copy(src, outs[j - 1].at[:, pl.ds(i * wide, wide)], sem.at[j - 1, i]))
    for cp in copies:
        cp.start()
    for cp in copies:
        cp.wait()


def deal(rows):
    hbm = pl.BlockSpec(memory_space=pl.ANY)
    shape = jax.ShapeDtypeStruct((rows.shape[0], rows.shape[1] // 4), BF16)
    return pl.pallas_call(
        deal_kernel, out_shape=[shape] * 3, in_specs=[hbm], out_specs=[hbm] * 3,
        scratch_shapes=[pltpu.SemaphoreType.DMA((3, 4))], name="deal",
    )(rows)


def local(input_rows, queries, key_values, out_grad, item_logratio, pair_ids, tile_item, tile_image):
    rows = input_rows[0]
    others = []
    for dx, block in zip(range(1, 4), deal(rows)):
        others.append(lax.ppermute(block, "tp", [(a, (a + 4 * dx) % 16) for a in range(16)]))
    dq, kvt = attention(queries, out_grad, key_values, item_logratio, pair_ids, tile_item, tile_image)
    return dq, exchange(kvt, rows, others).T


def solution(mesh):
    in_specs = (P("dp", "tp", None), P("dp", None, "tp"), P("dp", None, None), P("dp", None, "tp"),
                P("dp", None), P("dp", None), P("dp", None), P("dp", None))
    out_specs = (P("dp", None, "tp"), P("dp", "tp"))
    return jax.shard_map(local, mesh=mesh, in_specs=in_specs, out_specs=out_specs, check_vma=False)
```

profile of v0, /device:TPU:1, one launch (start us, length us, event | category | flops | bytes accessed | tf_op | source)
XLA Modules:
  0.0 93.6 jit_solution(9481337394707908426)
XLA Ops:
  0.6 25.0 %deal.1 = (bf16[128,1024]{1,0:T(8,128)(2,1)}, bf16[128,1024]{1,0:T(8,128)(2,1)}, bf16[128,1024]{1,0:T(8,128)(2,1)}) custom-call(bf16[128,4096]{1,0:T(8,128)(2,1)} %bitcast.2), custom_call_target="tpu_custom_call" | custom-call | tf_op jit(solution)/shard_map/deal/pallas_call | solution.py:464
  25.7 2.1 %collective-permute-start = (bf16[128,1024]{1,0:T(8,128)(2,1)}, bf16[128,1024]{1,0:T(8,128)(2,1)S(1)}, u32[]{:S(2)}, u32[]{:S(2)}) collective-permute-start(bf16[128,1024]{1,0:T(8,128)(2,1)} %get-tuple-element.9), channel_id=1, source_target_pairs={{0,4},{1,5},{2,6},{3,7},{4,8},{5,9},{6,10},{7,11},{8,12},{9,13},{1... | collective-permute-start | bytes 786440 | tf_op jit(solution)/shard_map/ppermute | solution.py:474
  27.8 2.5 %collective-permute-start.1 = (bf16[128,1024]{1,0:T(8,128)(2,1)}, bf16[128,1024]{1,0:T(8,128)(2,1)S(1)}, u32[]{:S(2)}, u32[]{:S(2)}) collective-permute-start(bf16[128,1024]{1,0:T(8,128)(2,1)} %get-tuple-element.10), channel_id=1, source_target_pairs={{0,8},{1,9},{2,10},{3,11},{4,12},{5,13},{6,14},{7,15},{8,0},{9,1},... | collective-permute-start | bytes 786440 | tf_op jit(solution)/shard_map/ppermute | solution.py:474
  30.3 1.2 %collective-permute-start.2 = (bf16[128,1024]{1,0:T(8,128)(2,1)}, bf16[128,1024]{1,0:T(8,128)(2,1)S(1)}, u32[]{:S(2)}, u32[]{:S(2)}) collective-permute-start(bf16[128,1024]{1,0:T(8,128)(2,1)} %get-tuple-element.11), channel_id=1, source_target_pairs={{0,12},{1,13},{2,14},{3,15},{4,0},{5,1},{6,2},{7,3},{8,4},{9,5},{1... | collective-permute-start | bytes 786440 | tf_op jit(solution)/shard_map/ppermute | solution.py:474
  31.4 13.9 %attention.1 = (bf16[1,2048,256]{2,1,0:T(8,128)(2,1)}, bf16[2,2,128,1024]{3,2,1,0:T(8,128)(2,1)}) custom-call(f32[1,4]{1,0:T(1,128)} %ratio_h.1, s32[1,4]{1,0:T(1,128)} %pair_h.1, s32[1,16]{1,0:T(1,128)} %item_h.1, s32[1,16]{1,0:T(1,128)} %image_h.1, bf16[1,2048,256]{2,1,0:T(8,128)(2,1)} %q_hbm.1, bf16[1,2048,256]{2,1,0:T(8,128)(2,1)} %og_hbm.1, ...), custom_call_target="tpu_custom_call" | custom-call | flops 10000000000 | bytes 8388608 | tf_op jit(solution)/shard_map/attention/pallas_call | solution.py:193
  45.3 0.0 collective-permute-done.x1
  45.3 0.0 copy-start
  45.3 0.0 collective-permute-done.1.x2
  45.3 0.0 copy-start.1
  45.3 0.0 collective-permute-done.2.x3
  45.3 0.0 copy-start.2
  45.3 0.7 copy-done
  46.0 0.1 copy-done.1
  46.1 0.1 copy-done.2
  46.2 45.9 %exchange.1 = f32[64,256]{1,0:T(8,128)} custom-call(bf16[2,2,128,1024]{3,2,1,0:T(8,128)(2,1)} %get-tuple-element.8.kvt, bf16[128,4096]{1,0:T(8,128)(2,1)} %bitcast.3, bf16[128,1024]{1,0:T(8,128)(2,1)} %copy-done, bf16[128,1024]{1,0:T(8,128)(2,1)} %copy-done.1, bf16[128,1024]{1,0:T(8,128)(2,1)} %copy-done.2), custom_call_target="tpu_custom_call" | custom-call | flops 1000000000 | bytes 8388608 | tf_op jit(solution)/shard_map/exchange/pallas_call | solution.py:425
  92.1 1.5 %copy.11 = f32[256,64]{0,1:T(8,128)} copy(f32[256,64]{0,1:T(8,128)} %bitcast.4) | data formatting | bytes 131072
Async XLA Ops:
  25.7 19.6 %collective-permute-start = (bf16[128,1024]{1,0:T(8,128)(2,1)}, bf16[128,1024]{1,0:T(8,128)(2,1)S(1)}, u32[]{:S(2)}, u32[]{:S(2)}) collective-permute-start(bf16[128,1024]{1,0:T(8,128)(2,1)} %get-tuple-element.9), channel_id=1, source_target_pairs={{0,4},{1,5},{2,6},{3,7},{4,8},{5,9},{6,10},{7,11},{8,12},{9,13},{1... | collective-permute-start | bytes 786440 | tf_op jit(solution)/shard_map/ppermute | solution.py:474
  27.8 17.5 %collective-permute-start.1 = (bf16[128,1024]{1,0:T(8,128)(2,1)}, bf16[128,1024]{1,0:T(8,128)(2,1)S(1)}, u32[]{:S(2)}, u32[]{:S(2)}) collective-permute-start(bf16[128,1024]{1,0:T(8,128)(2,1)} %get-tuple-element.10), channel_id=1, source_target_pairs={{0,8},{1,9},{2,10},{3,11},{4,12},{5,13},{6,14},{7,15},{8,0},{9,1},... | collective-permute-start | bytes 786440 | tf_op jit(solution)/shard_map/ppermute | solution.py:474
  30.3 15.1 %collective-permute-start.2 = (bf16[128,1024]{1,0:T(8,128)(2,1)}, bf16[128,1024]{1,0:T(8,128)(2,1)S(1)}, u32[]{:S(2)}, u32[]{:S(2)}) collective-permute-start(bf16[128,1024]{1,0:T(8,128)(2,1)} %get-tuple-element.11), channel_id=1, source_target_pairs={{0,12},{1,13},{2,14},{3,15},{4,0},{5,1},{6,2},{7,3},{8,4},{9,5},{1... | collective-permute-start | bytes 786440 | tf_op jit(solution)/shard_map/ppermute | solution.py:474
  45.3 0.7 copy-start
  45.3 0.8 copy-start.1
  45.3 0.9 copy-start.2
where the time goes:
time: 93.7 us; the launch traced here: 93.6 us
  Pallas kernels  84.8 us (91%)
  starting transfers between devices  5.72 us (6%)
  local copies, waits for them, and re-layouts  2.35 us (3%)
    pallas_call x1, Pallas kernels, exchange(): pl.pallas_call(exchange_kernel, out_shape=jax.ShapeDtypeStruct((PARTS * r...  45.9 us
    pallas_call x1, Pallas kernels, deal(): pl.pallas_call(deal_kernel, out_shape=[shape] * 3, in_specs=[hbm], out_sp...  25 us
    pallas_call x1, Pallas kernels, attention(): pl.pallas_call(attention_kernel, out_shape=[jax.ShapeDtypeStruct(queries....  13.9 us
    ppermute x3, starting transfers between devices, local(): lax.ppermute(block, 'tp', [(a, (a + 4 * dx) % 16) for a in range(16)])  5.72 us
    unnamed x7, local copies, waits for them, and re-layouts  2.35 us
  transfers between devices with their start and end apart: 3, of which 0 were waited for; matrix products, arithmetic and copies ran while one was open for 0% of the time, Pallas kernels for 15%

commit v1 on v0

--- a/solution.py
+++ b/solution.py
@@ -249,23 +249,10 @@
     load = pltpu.make_async_copy(kvt.at[c], own, load_sem)
     load.start()
     x_loads = []
-    wide = cols // 4
-
-    def piece(j, i):
-        return x_own.at[:, pl.ds(pl.multiple_of((4 * i + lax.rem(x + j, 4)) * wide, wide), wide)]
-
-    def place(i):
-        return xs.at[x, c, :, pl.ds(i * wide, wide)]
-
-    for i in range(4):
-        cp = pltpu.make_async_copy(piece(0, i), place(i), x_sem.at[i])
+    for j, src in enumerate((x_own, x1, x2, x3)):
+        cp = pltpu.make_async_copy(src, xs.at[lax.rem(x + 4 - j, 4), c], x_sem.at[j])
         cp.start()
         x_loads.append(cp)
-    xa = [None]
-    for j, src in enumerate((x1, x2, x3)):
-        cp = pltpu.make_async_copy(src, xs.at[lax.rem(x + 3 - j, 4), c], x_sem.at[4 + j])
-        cp.start()
-        xa.append([cp])
 
     barrier = pltpu.get_barrier_semaphore()
     for partner in (sibling, across, *beside[1:], *around[1:]):
@@ -308,8 +295,7 @@
     zc, rc, lc, frc, flc, yc, tc, xc = ([] for _ in range(8))
 
     def share(j):
-        for cp in xa[j] or x_loads:
-            cp.wait()
+        x_loads[j].wait()
         here = xs.at[lax.rem(x + 4 - j, 4), c]
         xc.append(send(here, here, xs_s.at[j], xs_r.at[j], sibling))
 
@@ -341,6 +327,7 @@
                 cp.wait_recv()
         lhs = heads[k].reshape(4 * rows, length)
         res = jnp.dot(lhs, xs[...].reshape(length, cols), preferred_element_type=F32)
+        wide = cols // 4
         for q in range(4):
             prod[k, q] = res[:, q * wide:(q + 1) * wide]
         sent = []
@@ -418,7 +405,7 @@
 
 def exchange(kvt, x_own, others):
     length = kvt.shape[3]
-    cols = x_own.shape[1] // 4
+    cols = x_own.shape[1]
     rows = HD // CHUNKS
     sem = pltpu.SemaphoreType.DMA
     n = CHUNKS
@@ -435,45 +422,37 @@
             pltpu.VMEM((n, 3, 4 * rows, cols // 4), BF16), pltpu.VMEM((n, 3, 4 * rows, cols // 4), BF16),
             pltpu.VMEM((n, 4, rows, cols // 4), BF16), pltpu.VMEM((n, 4, rows, cols // 4), BF16),
             pltpu.VMEM((8, PARTS, rows, cols // 4), BF16),
-        ] + [sem((n,))] * 12 + [sem((n, 3))] * 2 + [sem, sem((7,)), sem((4,)), sem((4,)),
+        ] + [sem((n,))] * 12 + [sem((n, 3))] * 2 + [sem, sem((4,)), sem((4,)), sem((4,)),
                                                     sem((n, 3)), sem((n, 3)), sem((4 * n,)), sem((8, PARTS))],
-        compiler_params=pltpu.CompilerParams(collective_id=0, has_side_effects=True, vmem_limit_bytes=56 << 20),
+        compiler_params=pltpu.CompilerParams(collective_id=0, has_side_effects=True, vmem_limit_bytes=40 << 20),
         cost_estimate=pl.CostEstimate(flops=10**9, bytes_accessed=8 << 20, transcendentals=0),
         name="exchange",
     )(kvt, x_own, *others)
 
 
-def deal_kernel(x_in, *rest):
-    outs, sem = rest[:3], rest[3]
+def deal_kernel(x_in, *outs):
     x = lax.axis_index("tp") // 4
     wide = outs[0].shape[1] // 4
-    copies = []
-    for j in range(1, 4):
+    for j in range(4):
         for i in range(4):
-            src = x_in.at[:, pl.ds(pl.multiple_of((4 * i + lax.rem(x + j, 4)) * wide, wide), wide)]
-            copies.append(pltpu.make_async_copy(src, outs[j - 1].at[:, pl.ds(i * wide, wide)], sem.at[j - 1, i]))
-    for cp in copies:
-        cp.start()
-    for cp in copies:
-        cp.wait()
+            cols = pl.ds(pl.multiple_of((4 * i + lax.rem(x + j, 4)) * wide, wide), wide)
+            outs[j][:, i * wide:(i + 1) * wide] = x_in[:, cols]
 
 
 def deal(rows):
-    hbm = pl.BlockSpec(memory_space=pl.ANY)
+    vmem = pl.BlockSpec(memory_space=pltpu.VMEM)
     shape = jax.ShapeDtypeStruct((rows.shape[0], rows.shape[1] // 4), BF16)
-    return pl.pallas_call(
-        deal_kernel, out_shape=[shape] * 3, in_specs=[hbm], out_specs=[hbm] * 3,
-        scratch_shapes=[pltpu.SemaphoreType.DMA((3, 4))], name="deal",
-    )(rows)
+    return pl.pallas_call(deal_kernel, out_shape=[shape] * 4, in_specs=[vmem], out_specs=[vmem] * 4, name="deal")(rows)
 
 
 def local(input_rows, queries, key_values, out_grad, item_logratio, pair_ids, tile_item, tile_image):
     rows = input_rows[0]
     others = []
-    for dx, block in zip(range(1, 4), deal(rows)):
+    mine, *blocks = deal(rows)
+    for dx, block in zip(range(1, 4), blocks):
         others.append(lax.ppermute(block, "tp", [(a, (a + 4 * dx) % 16) for a in range(16)]))
     dq, kvt = attention(queries, out_grad, key_values, item_logratio, pair_ids, tile_item, tile_image)
-    return dq, exchange(kvt, rows, others).T
+    return dq, exchange(kvt, mine, others).T
 
 
 def solution(mesh):

time: 93.7 us -> 73.8 us (0.79)
  Pallas kernels: 84.8 us -> 65.4 us
    pallas_call x1, Pallas kernels: 25 us -> 2.41 us  [deal(): pl.pallas_call(deal_kernel, out_shape=[shape] * 4, in_specs=[vmem], out_s...]
    pallas_call x1, Pallas kernels: 45.9 us -> 48.1 us  [exchange(): pl.pallas_call(exchange_kernel, out_shape=jax.ShapeDtypeStruct((PARTS * r...]
    pallas_call x1, Pallas kernels: 13.9 us -> 14.9 us  [attention(): pl.pallas_call(attention_kernel, out_shape=[jax.ShapeDtypeStruct(queries....]
    unnamed x7 -> x5, local copies, waits for them, and re-layouts: 2.35 us -> 1.85 us
  transfers between devices with their start and end apart: 3 -> 3, of which waited for: 0 -> 0; matrix products, arithmetic and copies ran while one was open for 0% -> 0% of each run, Pallas kernels for 15% -> 20%
where the time goes in v1:
time: 73.8 us; the launch traced here: 73.6 us
  Pallas kernels  65.4 us (89%)
  starting transfers between devices  5.64 us (8%)
  local copies, waits for them, and re-layouts  1.85 us (3%)
    pallas_call x1, Pallas kernels, exchange(): pl.pallas_call(exchange_kernel, out_shape=jax.ShapeDtypeStruct((PARTS * r...  48.1 us
    pallas_call x1, Pallas kernels, attention(): pl.pallas_call(attention_kernel, out_shape=[jax.ShapeDtypeStruct(queries....  14.9 us
    ppermute x3, starting transfers between devices, local(): lax.ppermute(block, 'tp', [(a, (a + 4 * dx) % 16) for a in range(16)])  5.64 us
    pallas_call x1, Pallas kernels, deal(): pl.pallas_call(deal_kernel, out_shape=[shape] * 4, in_specs=[vmem], out_s...  2.41 us
    unnamed x5, local copies, waits for them, and re-layouts  1.85 us
  transfers between devices with their start and end apart: 3, of which 0 were waited for; matrix products, arithmetic and copies ran while one was open for 0% of the time, Pallas kernels for 20%

profile of v1, /device:TPU:1, one launch (start us, length us, event | category | flops | bytes accessed | tf_op | source)
XLA Modules:
  0.0 73.6 jit_solution(3741148356969185743)
XLA Ops:
  0.6 2.4 %deal.1 = (bf16[128,1024]{1,0:T(8,128)(2,1)}, bf16[128,1024]{1,0:T(8,128)(2,1)}, bf16[128,1024]{1,0:T(8,128)(2,1)}, bf16[128,1024]{1,0:T(8,128)(2,1)}) custom-call(bf16[128,4096]{1,0:T(8,128)(2,1)} %bitcast.3), custom_call_target="tpu_custom_call" | custom-call | tf_op jit(solution)/shard_map/deal/pallas_call | solution.py:445
  3.0 2.0 %collective-permute-start = (bf16[128,1024]{1,0:T(8,128)(2,1)}, bf16[128,1024]{1,0:T(8,128)(2,1)S(1)}, u32[]{:S(2)}, u32[]{:S(2)}) collective-permute-start(bf16[128,1024]{1,0:T(8,128)(2,1)} %get-tuple-element.11), channel_id=1, source_target_pairs={{0,4},{1,5},{2,6},{3,7},{4,8},{5,9},{6,10},{7,11},{8,12},{9,13},{1... | collective-permute-start | bytes 786440 | tf_op jit(solution)/shard_map/ppermute | solution.py:453
  5.1 2.5 %collective-permute-start.1 = (bf16[128,1024]{1,0:T(8,128)(2,1)}, bf16[128,1024]{1,0:T(8,128)(2,1)S(1)}, u32[]{:S(2)}, u32[]{:S(2)}) collective-permute-start(bf16[128,1024]{1,0:T(8,128)(2,1)} %get-tuple-element.12), channel_id=1, source_target_pairs={{0,8},{1,9},{2,10},{3,11},{4,12},{5,13},{6,14},{7,15},{8,0},{9,1},... | collective-permute-start | bytes 786440 | tf_op jit(solution)/shard_map/ppermute | solution.py:453
  7.5 0.0 copy-start
  7.5 1.2 %collective-permute-start.2 = (bf16[128,1024]{1,0:T(8,128)(2,1)}, bf16[128,1024]{1,0:T(8,128)(2,1)S(1)}, u32[]{:S(2)}, u32[]{:S(2)}) collective-permute-start(bf16[128,1024]{1,0:T(8,128)(2,1)} %get-tuple-element.13), channel_id=1, source_target_pairs={{0,12},{1,13},{2,14},{3,15},{4,0},{5,1},{6,2},{7,3},{8,4},{9,5},{1... | collective-permute-start | bytes 786440 | tf_op jit(solution)/shard_map/ppermute | solution.py:453
  8.7 14.9 %attention.1 = (bf16[1,2048,256]{2,1,0:T(8,128)(2,1)}, bf16[2,2,128,1024]{3,2,1,0:T(8,128)(2,1)}) custom-call(f32[1,4]{1,0:T(1,128)} %ratio_h.1, s32[1,4]{1,0:T(1,128)} %pair_h.1, s32[1,16]{1,0:T(1,128)} %item_h.1, s32[1,16]{1,0:T(1,128)} %image_h.1, bf16[1,2048,256]{2,1,0:T(8,128)(2,1)} %q_hbm.1, bf16[1,2048,256]{2,1,0:T(8,128)(2,1)} %og_hbm.1, ...), custom_call_target="tpu_custom_call" | custom-call | flops 10000000000 | bytes 8388608 | tf_op jit(solution)/shard_map/attention/pallas_call | solution.py:193
  23.6 0.0 collective-permute-done.x1
  23.6 0.0 collective-permute-done.1.x2
  23.6 0.0 collective-permute-done.2.x3
  23.7 0.0 copy-done
  23.7 0.0 copy-start.1
  23.7 1.2 %copy-done.1 = bf16[2,2,128,1024]{3,2,1,0:T(8,128)(2,1)S(1)} copy-done((bf16[2,2,128,1024]{3,2,1,0:T(8,128)(2,1)S(1)}, bf16[2,2,128,1024]{3,2,1,0:T(8,128)(2,1)}, u32[]{:S(2)}) %copy-start.1) | copy-done | bytes 1048600
  24.9 48.1 %exchange.1 = f32[64,256]{1,0:T(8,128)S(1)} custom-call(bf16[2,2,128,1024]{3,2,1,0:T(8,128)(2,1)S(1)} %copy-done.1, bf16[128,1024]{1,0:T(8,128)(2,1)S(1)} %copy-done, bf16[128,1024]{1,0:T(8,128)(2,1)S(1)} %collective-permute-done.x1, bf16[128,1024]{1,0:T(8,128)(2,1)S(1)} %collective-permute-done.1.x2, bf16[128,1024]{1,0:T(8,128)(2,1)S(1)} %collective-permute-done.2.x3), custom_call_target="tpu_custom_call" | custom-call | flops 1000000000 | bytes 8388608 | tf_op jit(solution)/shard_map/exchange/pallas_call | solution.py:412
  73.0 0.6 copy.11
Async XLA Ops:
  3.0 20.6 %collective-permute-start = (bf16[128,1024]{1,0:T(8,128)(2,1)}, bf16[128,1024]{1,0:T(8,128)(2,1)S(1)}, u32[]{:S(2)}, u32[]{:S(2)}) collective-permute-start(bf16[128,1024]{1,0:T(8,128)(2,1)} %get-tuple-element.11), channel_id=1, source_target_pairs={{0,4},{1,5},{2,6},{3,7},{4,8},{5,9},{6,10},{7,11},{8,12},{9,13},{1... | collective-permute-start | bytes 786440 | tf_op jit(solution)/shard_map/ppermute | solution.py:453
  5.1 18.6 %collective-permute-start.1 = (bf16[128,1024]{1,0:T(8,128)(2,1)}, bf16[128,1024]{1,0:T(8,128)(2,1)S(1)}, u32[]{:S(2)}, u32[]{:S(2)}) collective-permute-start(bf16[128,1024]{1,0:T(8,128)(2,1)} %get-tuple-element.12), channel_id=1, source_target_pairs={{0,8},{1,9},{2,10},{3,11},{4,12},{5,13},{6,14},{7,15},{8,0},{9,1},... | collective-permute-start | bytes 786440 | tf_op jit(solution)/shard_map/ppermute | solution.py:453
  7.5 16.1 %copy-start = (bf16[128,1024]{1,0:T(8,128)(2,1)S(1)}, bf16[128,1024]{1,0:T(8,128)(2,1)}, u32[]{:S(2)}) copy-start(bf16[128,1024]{1,0:T(8,128)(2,1)} %get-tuple-element.10.x_own) | copy-start | bytes 786436
  7.5 16.1 %collective-permute-start.2 = (bf16[128,1024]{1,0:T(8,128)(2,1)}, bf16[128,1024]{1,0:T(8,128)(2,1)S(1)}, u32[]{:S(2)}, u32[]{:S(2)}) collective-permute-start(bf16[128,1024]{1,0:T(8,128)(2,1)} %get-tuple-element.13), channel_id=1, source_target_pairs={{0,12},{1,13},{2,14},{3,15},{4,0},{5,1},{6,2},{7,3},{8,4},{9,5},{1... | collective-permute-start | bytes 786440 | tf_op jit(solution)/shard_map/ppermute | solution.py:453
  23.7 1.2 %copy-start.1 = (bf16[2,2,128,1024]{3,2,1,0:T(8,128)(2,1)S(1)}, bf16[2,2,128,1024]{3,2,1,0:T(8,128)(2,1)}, u32[]{:S(2)}) copy-start(bf16[2,2,128,1024]{3,2,1,0:T(8,128)(2,1)} %get-tuple-element.9.kvt) | copy-start | bytes 3145732

commit v2 on v1

--- a/solution.py
+++ b/solution.py
@@ -12,7 +12,7 @@
 
 def attention_kernel(ratio_h, pair_h, item_h, image_h, q_hbm, og_hbm, kv_hbm, dq_hbm, kvt_ref,
                      kv, q_ref, og_ref, dq_ref, s0, s1, dp0, dp1, acc, ratio, pair, item, image,
-                     lo_s, hi_s, n_s, order, work, z_s, small_sem, big_sem, dq_sem):
+                     lo_s, hi_s, n_s, spot, order, work, z_s, small_sem, big_sem, dq_sem):
     group = lax.axis_size("tp") // KVH
     g = lax.axis_index("tp") // group
     nt = item.shape[1]
@@ -54,12 +54,18 @@
     for i in range(nt):
         n_s[i] = (hi_s[i] - lo_s[i] + 2) // 2
 
-    def place(t, pos):
-        i = lax.rem(t, nt)
-        order[pos] = i
-        return pos + jnp.where(n_s[i] == nt // 2 - t // nt, 1, 0)
-
-    lax.fori_loop(0, nt * nt // 2, place, jnp.int32(0))
+    for n in range(nt // 2 + 1):
+        spot[n] = 0
+    for i in range(nt):
+        spot[n_s[i]] = spot[n_s[i]] + 1
+    start = jnp.int32(0)
+    for n in reversed(range(1, nt // 2 + 1)):
+        here = spot[n]
+        spot[n] = start
+        start = start + here
+    for i in range(nt):
+        order[spot[n_s[i]]] = i
+        spot[n_s[i]] = spot[n_s[i]] + 1
 
     def match(t, carry):
         i, w = carry
@@ -104,8 +110,7 @@
                 s = lax.dot_general(q2, kv[rows, :HD], (((1,), (1,)), ((), ())), preferred_element_type=jnp.float32)
                 if ch <= spare or ch >= n - 2:
                     col = lax.broadcasted_iota(jnp.int32, (1, W), 1) + ch * W
-                    ok = (col <= last) & (col >= first)
-                    s = jnp.where(ok, s, MASKED)
+                    s = jnp.where(jnp.where(col >= first, col, nt * TILE) <= last, s, MASKED)
                 s_scr[:, ch * W:(ch + 1) * W] = s
                 mm = jnp.maximum(s[:, :HD], s[:, HD:])
                 m = mm if m is None else jnp.maximum(m, mm)
@@ -205,6 +210,7 @@
             pltpu.SMEM((nt,), jnp.int32),
             pltpu.SMEM((nt,), jnp.int32),
             pltpu.SMEM((nt,), jnp.int32),
+            pltpu.SMEM((nt // 2 + 1,), jnp.int32),
             pltpu.SMEM((nt + 1,), jnp.int32),
             pltpu.SMEM((3 * (nt + 1),), jnp.int32),
             pltpu.SMEM((2 * ratio.shape[1],), jnp.float32),
@@ -218,7 +224,7 @@
 
 CHUNKS = 4
 PARTS = CHUNKS // 2
-TIMES = ((0, 1), (1, 1), (2.2, 1), (3.3, 1), (5.4, 1), (6.5, 1))
+TIMES = ((0, 1), (1, 1), (3.2, 1), (5.4, 1), (7.5, 1))
 SHARE = (0.5, 0.5, 0.5, 0.5)
 MESH = pl.DeviceIdType.MESH
 F32 = jnp.float32
@@ -227,8 +233,7 @@
 
 def exchange_kernel(kvt, x_own, x1, x2, x3, out_ref,
                     own, core_in, part, z_in, heads, xs, prod, y_out, y_in, final, turned, landed,
-                    core_s, core_r, z_s, z_r, right_s, right_r, left_s, left_r,
-                    fr_s, fr_r, fl_s, fl_r, y_s, y_r,
+                    core_s, core_r, z_s, z_r, x_s, x_r, y_s, y_r,
                     load_sem, x_sem, xs_s, xs_r, turn_s, turn_r, out_s, out_r):
     dp = lax.axis_index("dp")
     tp = lax.axis_index("tp")
@@ -239,12 +244,10 @@
     c = tp % 2
     rows, length = z_in.shape[1:]
     cols = xs.shape[3]
-    half = length // 2
     sibling = (dp, x * 4 + zl * 2 + (1 - c))
     across = (dp, x * 4 + (1 - zl) * 2 + c)
     around = [(lax.rem(y + j, 4) * 4 + zh, tp) for j in range(4)]
     beside = [(dp, lax.rem(x + j, 4) * 4 + zl * 2 + c) for j in range(4)]
-    right, left = beside[1], beside[3]
 
     load = pltpu.make_async_copy(kvt.at[c], own, load_sem)
     load.start()
@@ -292,7 +295,7 @@
             for k in range(CHUNKS)]
     load.wait()
 
-    zc, rc, lc, frc, flc, yc, tc, xc = ([] for _ in range(8))
+    zc, hc, yc, tc, xc = ([] for _ in range(5))
 
     def share(j):
         x_loads[j].wait()
@@ -308,20 +311,11 @@
         zc[k].wait_recv()
         heads[k, x] = (own[zl, cut(k)].astype(F32) + core_in[k, zl].astype(F32) + z_in[k].astype(F32)).astype(BF16)
         here = heads.at[k, x]
-        rc.append(send(here, here, right_s.at[k], right_r.at[k], right))
-        lc.append(send(here, here, left_s.at[k], left_r.at[k], left))
-
-    def forward(k):
-        rc[k].wait_recv()
-        a = heads.at[k, lax.rem(x + 3, 4), :, pl.ds(0, half)]
-        frc.append(send(a, a, fr_s.at[k], fr_r.at[k], right))
-        lc[k].wait_recv()
-        b = heads.at[k, lax.rem(x + 1, 4), :, pl.ds(half, half)]
-        flc.append(send(b, b, fl_s.at[k], fl_r.at[k], left))
+        hc.append([send(here, here, x_s.at[k, j - 1], x_r.at[k, j - 1], beside[j]) for j in (2, 1, 3)])
 
     def multiply(k):
-        frc[k].wait_recv()
-        flc[k].wait_recv()
+        for cp in hc[k]:
+            cp.wait_recv()
         if k == 0:
             for cp in xc:
                 cp.wait_recv()
@@ -372,7 +366,7 @@
             return carry
         lax.fori_loop(0, 4, one, 0)
 
-    stages = (reduce_core, reduce_z, forward, multiply, deliver, scatter)
+    stages = (reduce_core, reduce_z, multiply, deliver, scatter)
     order = sorted((start + k * gap, i, k) for i, (start, gap) in enumerate(TIMES) for k in range(CHUNKS))
     order = sorted(order + [(SHARE[j], -1, j) for j in range(4)])
     for _, i, k in order:
@@ -422,7 +416,7 @@
             pltpu.VMEM((n, 3, 4 * rows, cols // 4), BF16), pltpu.VMEM((n, 3, 4 * rows, cols // 4), BF16),
             pltpu.VMEM((n, 4, rows, cols // 4), BF16), pltpu.VMEM((n, 4, rows, cols // 4), BF16),
             pltpu.VMEM((8, PARTS, rows, cols // 4), BF16),
-        ] + [sem((n,))] * 12 + [sem((n, 3))] * 2 + [sem, sem((4,)), sem((4,)), sem((4,)),
+        ] + [sem((n,))] * 4 + [sem((n, 3))] * 4 + [sem, sem((4,)), sem((4,)), sem((4,)),
                                                     sem((n, 3)), sem((n, 3)), sem((4 * n,)), sem((8, PARTS))],
         compiler_params=pltpu.CompilerParams(collective_id=0, has_side_effects=True, vmem_limit_bytes=40 << 20),
         cost_estimate=pl.CostEstimate(flops=10**9, bytes_accessed=8 << 20, transcendentals=0),

time: 73.8 us -> 68.7 us (0.931)
  Pallas kernels: 65.4 us -> 60.3 us
    pallas_call x1, Pallas kernels: 48.1 us -> 45 us  [exchange(): pl.pallas_call(exchange_kernel, out_shape=jax.ShapeDtypeStruct((PARTS * r...]
    pallas_call x1, Pallas kernels: 14.9 us -> 12.9 us  [attention(): pl.pallas_call(attention_kernel, out_shape=[jax.ShapeDtypeStruct(queries....]
  transfers between devices with their start and end apart: 3 -> 3, of which waited for: 0 -> 0; matrix products, arithmetic and copies ran while one was open for 0% -> 0% of each run, Pallas kernels for 20% -> 19%
where the time goes in v2:
time: 68.7 us; the launch traced here: 68.5 us
  Pallas kernels  60.3 us (88%)
  starting transfers between devices  5.64 us (8%)
  local copies, waits for them, and re-layouts  1.85 us (3%)
  between operations  0.69 us (1%)
    pallas_call x1, Pallas kernels, exchange(): pl.pallas_call(exchange_kernel, out_shape=jax.ShapeDtypeStruct((PARTS * r...  45 us
    pallas_call x1, Pallas kernels, attention(): pl.pallas_call(attention_kernel, out_shape=[jax.ShapeDtypeStruct(queries....  12.9 us
    ppermute x3, starting transfers between devices, local(): lax.ppermute(block, 'tp', [(a, (a + 4 * dx) % 16) for a in range(16)])  5.64 us
    pallas_call x1, Pallas kernels, deal(): pl.pallas_call(deal_kernel, out_shape=[shape] * 4, in_specs=[vmem], out_s...  2.41 us
    unnamed x5, local copies, waits for them, and re-layouts  1.85 us
  transfers between devices with their start and end apart: 3, of which 0 were waited for; matrix products, arithmetic and copies ran while one was open for 0% of the time, Pallas kernels for 19%

profile of v2, /device:TPU:1, one launch (start us, length us, event | category | flops | bytes accessed | tf_op | source)
XLA Modules:
  0.0 68.5 jit_solution(16830433832124492829)
XLA Ops:
  0.6 2.4 %deal.1 = (bf16[128,1024]{1,0:T(8,128)(2,1)}, bf16[128,1024]{1,0:T(8,128)(2,1)}, bf16[128,1024]{1,0:T(8,128)(2,1)}, bf16[128,1024]{1,0:T(8,128)(2,1)}) custom-call(bf16[128,4096]{1,0:T(8,128)(2,1)} %bitcast.3), custom_call_target="tpu_custom_call" | custom-call | tf_op jit(solution)/shard_map/deal/pallas_call | solution.py:439
  3.0 2.0 %collective-permute-start = (bf16[128,1024]{1,0:T(8,128)(2,1)}, bf16[128,1024]{1,0:T(8,128)(2,1)S(1)}, u32[]{:S(2)}, u32[]{:S(2)}) collective-permute-start(bf16[128,1024]{1,0:T(8,128)(2,1)} %get-tuple-element.11), channel_id=1, source_target_pairs={{0,4},{1,5},{2,6},{3,7},{4,8},{5,9},{6,10},{7,11},{8,12},{9,13},{1... | collective-permute-start | bytes 786440 | tf_op jit(solution)/shard_map/ppermute | solution.py:447
  5.1 2.5 %collective-permute-start.1 = (bf16[128,1024]{1,0:T(8,128)(2,1)}, bf16[128,1024]{1,0:T(8,128)(2,1)S(1)}, u32[]{:S(2)}, u32[]{:S(2)}) collective-permute-start(bf16[128,1024]{1,0:T(8,128)(2,1)} %get-tuple-element.12), channel_id=1, source_target_pairs={{0,8},{1,9},{2,10},{3,11},{4,12},{5,13},{6,14},{7,15},{8,0},{9,1},... | collective-permute-start | bytes 786440 | tf_op jit(solution)/shard_map/ppermute | solution.py:447
  7.5 0.0 copy-start
  7.5 1.2 %collective-permute-start.2 = (bf16[128,1024]{1,0:T(8,128)(2,1)}, bf16[128,1024]{1,0:T(8,128)(2,1)S(1)}, u32[]{:S(2)}, u32[]{:S(2)}) collective-permute-start(bf16[128,1024]{1,0:T(8,128)(2,1)} %get-tuple-element.13), channel_id=1, source_target_pairs={{0,12},{1,13},{2,14},{3,15},{4,0},{5,1},{6,2},{7,3},{8,4},{9,5},{1... | collective-permute-start | bytes 786440 | tf_op jit(solution)/shard_map/ppermute | solution.py:447
  8.7 12.9 %attention.1 = (bf16[1,2048,256]{2,1,0:T(8,128)(2,1)}, bf16[2,2,128,1024]{3,2,1,0:T(8,128)(2,1)}) custom-call(f32[1,4]{1,0:T(1,128)} %ratio_h.1, s32[1,4]{1,0:T(1,128)} %pair_h.1, s32[1,16]{1,0:T(1,128)} %item_h.1, s32[1,16]{1,0:T(1,128)} %image_h.1, bf16[1,2048,256]{2,1,0:T(8,128)(2,1)} %q_hbm.1, bf16[1,2048,256]{2,1,0:T(8,128)(2,1)} %og_hbm.1, ...), custom_call_target="tpu_custom_call" | custom-call | flops 10000000000 | bytes 8388608 | tf_op jit(solution)/shard_map/attention/pallas_call | solution.py:198
  21.6 0.0 collective-permute-done.x1
  21.6 0.0 collective-permute-done.1.x2
  21.6 0.0 collective-permute-done.2.x3
  21.6 0.0 copy-done
  21.6 0.0 copy-start.1
  21.6 1.2 %copy-done.1 = bf16[2,2,128,1024]{3,2,1,0:T(8,128)(2,1)S(1)} copy-done((bf16[2,2,128,1024]{3,2,1,0:T(8,128)(2,1)S(1)}, bf16[2,2,128,1024]{3,2,1,0:T(8,128)(2,1)}, u32[]{:S(2)}) %copy-start.1) | copy-done | bytes 1048600
  22.8 45.0 %exchange.1 = f32[64,256]{1,0:T(8,128)S(1)} custom-call(bf16[2,2,128,1024]{3,2,1,0:T(8,128)(2,1)S(1)} %copy-done.1, bf16[128,1024]{1,0:T(8,128)(2,1)S(1)} %copy-done, bf16[128,1024]{1,0:T(8,128)(2,1)S(1)} %collective-permute-done.x1, bf16[128,1024]{1,0:T(8,128)(2,1)S(1)} %collective-permute-done.1.x2, bf16[128,1024]{1,0:T(8,128)(2,1)S(1)} %collective-permute-done.2.x3), custom_call_target="tpu_custom_call" | custom-call | flops 1000000000 | bytes 8388608 | tf_op jit(solution)/shard_map/exchange/pallas_call | solution.py:406
  67.9 0.6 copy.11
Async XLA Ops:
  3.0 18.5 %collective-permute-start = (bf16[128,1024]{1,0:T(8,128)(2,1)}, bf16[128,1024]{1,0:T(8,128)(2,1)S(1)}, u32[]{:S(2)}, u32[]{:S(2)}) collective-permute-start(bf16[128,1024]{1,0:T(8,128)(2,1)} %get-tuple-element.11), channel_id=1, source_target_pairs={{0,4},{1,5},{2,6},{3,7},{4,8},{5,9},{6,10},{7,11},{8,12},{9,13},{1... | collective-permute-start | bytes 786440 | tf_op jit(solution)/shard_map/ppermute | solution.py:447
  5.1 16.5 %collective-permute-start.1 = (bf16[128,1024]{1,0:T(8,128)(2,1)}, bf16[128,1024]{1,0:T(8,128)(2,1)S(1)}, u32[]{:S(2)}, u32[]{:S(2)}) collective-permute-start(bf16[128,1024]{1,0:T(8,128)(2,1)} %get-tuple-element.12), channel_id=1, source_target_pairs={{0,8},{1,9},{2,10},{3,11},{4,12},{5,13},{6,14},{7,15},{8,0},{9,1},... | collective-permute-start | bytes 786440 | tf_op jit(solution)/shard_map/ppermute | solution.py:447
  7.5 14.1 %copy-start = (bf16[128,1024]{1,0:T(8,128)(2,1)S(1)}, bf16[128,1024]{1,0:T(8,128)(2,1)}, u32[]{:S(2)}) copy-start(bf16[128,1024]{1,0:T(8,128)(2,1)} %get-tuple-element.10.x_own) | copy-start | bytes 786436
  7.5 14.1 %collective-permute-start.2 = (bf16[128,1024]{1,0:T(8,128)(2,1)}, bf16[128,1024]{1,0:T(8,128)(2,1)S(1)}, u32[]{:S(2)}, u32[]{:S(2)}) collective-permute-start(bf16[128,1024]{1,0:T(8,128)(2,1)} %get-tuple-element.13), channel_id=1, source_target_pairs={{0,12},{1,13},{2,14},{3,15},{4,0},{5,1},{6,2},{7,3},{8,4},{9,5},{1... | collective-permute-start | bytes 786440 | tf_op jit(solution)/shard_map/ppermute | solution.py:447
  21.6 1.2 %copy-start.1 = (bf16[2,2,128,1024]{3,2,1,0:T(8,128)(2,1)S(1)}, bf16[2,2,128,1024]{3,2,1,0:T(8,128)(2,1)}, u32[]{:S(2)}) copy-start(bf16[2,2,128,1024]{3,2,1,0:T(8,128)(2,1)} %get-tuple-element.9.kvt) | copy-start | bytes 3145732

commit v3 on v2

--- a/solution.py
+++ b/solution.py
@@ -10,9 +10,9 @@
 MASKED = -1e30
 LOG2E = 1.4426950408889634
 
-def attention_kernel(ratio_h, pair_h, item_h, image_h, q_hbm, og_hbm, kv_hbm, dq_hbm, kvt_ref,
-                     kv, q_ref, og_ref, dq_ref, s0, s1, dp0, dp1, acc, ratio, pair, item, image,
-                     lo_s, hi_s, n_s, spot, order, work, z_s, small_sem, big_sem, dq_sem):
+def attention_kernel(ratio_h, pair_h, item_h, image_h, q_hbm, og_hbm, kv_hbm, dq_hbm, kvt_hbm,
+                     kvt_ref, kv, q_ref, og_ref, dq_ref, s0, s1, dp0, dp1, acc, ratio, pair, item, image,
+                     lo_s, hi_s, n_s, spot, order, work, z_s, small_sem, big_sem, dq_sem, kvt_sem):
     group = lax.axis_size("tp") // KVH
     g = lax.axis_index("tp") // group
     nt = item.shape[1]
@@ -176,17 +176,23 @@
         return carry
 
     lax.fori_loop(0, count, row_pair, 0)
-    for i in range(nt // 4):
+    kvt_out = []
+    for part in range(2):
         for z in range(2):
-            frm = slice((2 * i + z) * W, (2 * i + z + 1) * W)
-            to = slice(i * W, (i + 1) * W)
-            kvt_ref[0, z, :, to] = (acc[:HD, frm] * inv_root).astype(jnp.bfloat16)
-            kvt_ref[1, z, :, to] = acc[HD:, frm].astype(jnp.bfloat16)
+            for i in range(nt // 4):
+                frm = slice((2 * i + z) * W, (2 * i + z + 1) * W)
+                block = acc[part * HD:(part + 1) * HD, frm]
+                kvt_ref[part, z, :, i * W:(i + 1) * W] = (block if part else block * inv_root).astype(jnp.bfloat16)
+            cp = pltpu.make_async_copy(kvt_ref.at[part, z], kvt_hbm.at[part, z], kvt_sem.at[part, z])
+            cp.start()
+            kvt_out.append(cp)
 
     def finish(i, carry):
         out_copy(i).wait()
         return carry
     lax.fori_loop(0, nt, finish, 0)
+    for cp in kvt_out:
+        cp.wait()
 
 
 def attention(queries, out_grad, key_values, ratio, pair, item, image):
@@ -200,8 +206,8 @@
         out_shape=[jax.ShapeDtypeStruct(queries.shape, jnp.bfloat16),
                    jax.ShapeDtypeStruct((2, 2, HD, L // 2), jnp.bfloat16)],
         in_specs=[hbm] * 7,
-        out_specs=[hbm, pl.BlockSpec(memory_space=pltpu.VMEM)],
-        scratch_shapes=[low, low, low, pltpu.VMEM((L + TILE, 2 * HD), jnp.bfloat16), wide, wide, wide, wide,
+        out_specs=[hbm, hbm],
+        scratch_shapes=[pltpu.VMEM((2, 2, HD, L // 2), jnp.bfloat16), low, low, low, pltpu.VMEM((L + TILE, 2 * HD), jnp.bfloat16), wide, wide, wide, wide,
             pltpu.VMEM((2 * HD, L), jnp.float32),
             pltpu.SMEM(ratio.shape, jnp.float32),
             pltpu.SMEM(pair.shape, jnp.int32),
@@ -214,7 +220,7 @@
             pltpu.SMEM((nt + 1,), jnp.int32),
             pltpu.SMEM((3 * (nt + 1),), jnp.int32),
             pltpu.SMEM((2 * ratio.shape[1],), jnp.float32),
-            pltpu.SemaphoreType.DMA((4,)), pltpu.SemaphoreType.DMA((3,)), pltpu.SemaphoreType.DMA((nt,)),
+            pltpu.SemaphoreType.DMA((4,)), pltpu.SemaphoreType.DMA((3,)), pltpu.SemaphoreType.DMA((nt,)), pltpu.SemaphoreType.DMA((2, 2)),
         ],
         compiler_params=pltpu.CompilerParams(vmem_limit_bytes=56 << 20),
         cost_estimate=pl.CostEstimate(flops=10 * 10**9, bytes_accessed=8 << 20, transcendentals=0),
@@ -249,6 +255,27 @@
     around = [(lax.rem(y + j, 4) * 4 + zh, tp) for j in range(4)]
     beside = [(dp, lax.rem(x + j, 4) * 4 + zl * 2 + c) for j in range(4)]
 
+    barrier = pltpu.get_barrier_semaphore()
+    for partner in (sibling, across, *beside[1:], *around[1:]):
+        pl.semaphore_signal(barrier, 1, device_id=partner, device_id_type=MESH)
+
+    def dest(u, h):
+        return y * 4 + h, x * 4 + c * 2 + u
+
+    def is_other(d, t):
+        return jnp.logical_or(d != dp, t != tp)
+
+    def greet(d, t, n):
+        other = is_other(d, t)
+
+        @pl.when(other)
+        def _():
+            pl.semaphore_signal(barrier, 1, device_id=(d, t), device_id_type=MESH)
+        return n + jnp.where(other, 1, 0)
+
+    n = lax.fori_loop(0, 8, lambda i, n: greet(*dest(i % 2, i // 2), n), jnp.int32(8))
+    n = lax.fori_loop(0, 8, lambda i, n: greet(y * 4 + i // 2, x * 4 + i % 2 * 2 + zl, n), n)
+
     load = pltpu.make_async_copy(kvt.at[c], own, load_sem)
     load.start()
     x_loads = []
@@ -257,26 +284,6 @@
         cp.start()
         x_loads.append(cp)
 
-    barrier = pltpu.get_barrier_semaphore()
-    for partner in (sibling, across, *beside[1:], *around[1:]):
-        pl.semaphore_signal(barrier, 1, device_id=partner, device_id_type=MESH)
-
-    def dest(u, h):
-        return y * 4 + h, x * 4 + c * 2 + u
-
-    def is_other(d, t):
-        return jnp.logical_or(d != dp, t != tp)
-
-    def greet(d, t, n):
-        other = is_other(d, t)
-
-        @pl.when(other)
-        def _():
-            pl.semaphore_signal(barrier, 1, device_id=(d, t), device_id_type=MESH)
-        return n + jnp.where(other, 1, 0)
-
-    n = lax.fori_loop(0, 8, lambda i, n: greet(*dest(i % 2, i // 2), n), jnp.int32(8))
-    n = lax.fori_loop(0, 8, lambda i, n: greet(y * 4 + i // 2, x * 4 + i % 2 * 2 + zl, n), n)
     pl.semaphore_wait(barrier, n)
 
     started = []

time: 68.7 us -> 69.5 us (1.012)
  Pallas kernels: 60.3 us -> 61.7 us
    pallas_call x1, Pallas kernels: 45 us -> 46.5 us  [exchange(): pl.pallas_call(exchange_kernel, out_shape=jax.ShapeDtypeStruct((PARTS * r...]
  transfers between devices with their start and end apart: 3 -> 3, of which waited for: 0 -> 0; matrix products, arithmetic and copies ran while one was open for 0% -> 0% of each run, Pallas kernels for 19% -> 18%
where the time goes in v3:
time: 69.5 us; the launch traced here: 69.9 us
  Pallas kernels  61.7 us (89%)
  starting transfers between devices  5.64 us (8%)
  local copies, waits for them, and re-layouts  1.85 us (3%)
    pallas_call x1, Pallas kernels, exchange(): pl.pallas_call(exchange_kernel, out_shape=jax.ShapeDtypeStruct((PARTS * r...  46.5 us
    pallas_call x1, Pallas kernels, attention(): pl.pallas_call(attention_kernel, out_shape=[jax.ShapeDtypeStruct(queries....  12.9 us
    ppermute x3, starting transfers between devices, local(): lax.ppermute(block, 'tp', [(a, (a + 4 * dx) % 16) for a in range(16)])  5.64 us
    pallas_call x1, Pallas kernels, deal(): pl.pallas_call(deal_kernel, out_shape=[shape] * 4, in_specs=[vmem], out_s...  2.41 us
    unnamed x5, local copies, waits for them, and re-layouts  1.85 us
  transfers between devices with their start and end apart: 3, of which 0 were waited for; matrix products, arithmetic and copies ran while one was open for 0% of the time, Pallas kernels for 18%

profile of v3, /device:TPU:1, one launch (start us, length us, event | category | flops | bytes accessed | tf_op | source)
XLA Modules:
  0.0 69.9 jit_solution(1650367287176068624)
XLA Ops:
  0.6 2.4 %deal.1 = (bf16[128,1024]{1,0:T(8,128)(2,1)}, bf16[128,1024]{1,0:T(8,128)(2,1)}, bf16[128,1024]{1,0:T(8,128)(2,1)}, bf16[128,1024]{1,0:T(8,128)(2,1)}) custom-call(bf16[128,4096]{1,0:T(8,128)(2,1)} %bitcast.3), custom_call_target="tpu_custom_call" | custom-call | tf_op jit(solution)/shard_map/deal/pallas_call | solution.py:446
  3.0 2.0 %collective-permute-start = (bf16[128,1024]{1,0:T(8,128)(2,1)}, bf16[128,1024]{1,0:T(8,128)(2,1)S(1)}, u32[]{:S(2)}, u32[]{:S(2)}) collective-permute-start(bf16[128,1024]{1,0:T(8,128)(2,1)} %get-tuple-element.11), channel_id=1, source_target_pairs={{0,4},{1,5},{2,6},{3,7},{4,8},{5,9},{6,10},{7,11},{8,12},{9,13},{1... | collective-permute-start | bytes 786440 | tf_op jit(solution)/shard_map/ppermute | solution.py:454
  5.1 2.5 %collective-permute-start.1 = (bf16[128,1024]{1,0:T(8,128)(2,1)}, bf16[128,1024]{1,0:T(8,128)(2,1)S(1)}, u32[]{:S(2)}, u32[]{:S(2)}) collective-permute-start(bf16[128,1024]{1,0:T(8,128)(2,1)} %get-tuple-element.12), channel_id=1, source_target_pairs={{0,8},{1,9},{2,10},{3,11},{4,12},{5,13},{6,14},{7,15},{8,0},{9,1},... | collective-permute-start | bytes 786440 | tf_op jit(solution)/shard_map/ppermute | solution.py:454
  7.5 0.0 copy-start
  7.5 1.2 %collective-permute-start.2 = (bf16[128,1024]{1,0:T(8,128)(2,1)}, bf16[128,1024]{1,0:T(8,128)(2,1)S(1)}, u32[]{:S(2)}, u32[]{:S(2)}) collective-permute-start(bf16[128,1024]{1,0:T(8,128)(2,1)} %get-tuple-element.13), channel_id=1, source_target_pairs={{0,12},{1,13},{2,14},{3,15},{4,0},{5,1},{6,2},{7,3},{8,4},{9,5},{1... | collective-permute-start | bytes 786440 | tf_op jit(solution)/shard_map/ppermute | solution.py:454
  8.7 12.9 %attention.1 = (bf16[1,2048,256]{2,1,0:T(8,128)(2,1)}, bf16[2,2,128,1024]{3,2,1,0:T(8,128)(2,1)}) custom-call(f32[1,4]{1,0:T(1,128)} %ratio_h.1, s32[1,4]{1,0:T(1,128)} %pair_h.1, s32[1,16]{1,0:T(1,128)} %item_h.1, s32[1,16]{1,0:T(1,128)} %image_h.1, bf16[1,2048,256]{2,1,0:T(8,128)(2,1)} %q_hbm.1, bf16[1,2048,256]{2,1,0:T(8,128)(2,1)} %og_hbm.1, ...), custom_call_target="tpu_custom_call" | custom-call | flops 10000000000 | bytes 8388608 | tf_op jit(solution)/shard_map/attention/pallas_call | solution.py:204
  21.6 0.0 collective-permute-done.x1
  21.6 0.0 collective-permute-done.1.x2
  21.6 0.0 collective-permute-done.2.x3
  21.6 0.0 copy-done
  21.6 0.0 copy-start.1
  21.6 1.2 %copy-done.1 = bf16[2,2,128,1024]{3,2,1,0:T(8,128)(2,1)S(1)} copy-done((bf16[2,2,128,1024]{3,2,1,0:T(8,128)(2,1)S(1)}, bf16[2,2,128,1024]{3,2,1,0:T(8,128)(2,1)}, u32[]{:S(2)}) %copy-start.1) | copy-done | bytes 1048600
  22.8 46.5 %exchange.1 = f32[64,256]{1,0:T(8,128)S(1)} custom-call(bf16[2,2,128,1024]{3,2,1,0:T(8,128)(2,1)S(1)} %copy-done.1, bf16[128,1024]{1,0:T(8,128)(2,1)S(1)} %copy-done, bf16[128,1024]{1,0:T(8,128)(2,1)S(1)} %collective-permute-done.x1, bf16[128,1024]{1,0:T(8,128)(2,1)S(1)} %collective-permute-done.1.x2, bf16[128,1024]{1,0:T(8,128)(2,1)S(1)} %collective-permute-done.2.x3), custom_call_target="tpu_custom_call" | custom-call | flops 1000000000 | bytes 8388608 | tf_op jit(solution)/shard_map/exchange/pallas_call | solution.py:413
  69.3 0.6 copy.11
Async XLA Ops:
  3.0 18.5 %collective-permute-start = (bf16[128,1024]{1,0:T(8,128)(2,1)}, bf16[128,1024]{1,0:T(8,128)(2,1)S(1)}, u32[]{:S(2)}, u32[]{:S(2)}) collective-permute-start(bf16[128,1024]{1,0:T(8,128)(2,1)} %get-tuple-element.11), channel_id=1, source_target_pairs={{0,4},{1,5},{2,6},{3,7},{4,8},{5,9},{6,10},{7,11},{8,12},{9,13},{1... | collective-permute-start | bytes 786440 | tf_op jit(solution)/shard_map/ppermute | solution.py:454
  5.1 16.5 %collective-permute-start.1 = (bf16[128,1024]{1,0:T(8,128)(2,1)}, bf16[128,1024]{1,0:T(8,128)(2,1)S(1)}, u32[]{:S(2)}, u32[]{:S(2)}) collective-permute-start(bf16[128,1024]{1,0:T(8,128)(2,1)} %get-tuple-element.12), channel_id=1, source_target_pairs={{0,8},{1,9},{2,10},{3,11},{4,12},{5,13},{6,14},{7,15},{8,0},{9,1},... | collective-permute-start | bytes 786440 | tf_op jit(solution)/shard_map/ppermute | solution.py:454
  7.5 14.1 %copy-start = (bf16[128,1024]{1,0:T(8,128)(2,1)S(1)}, bf16[128,1024]{1,0:T(8,128)(2,1)}, u32[]{:S(2)}) copy-start(bf16[128,1024]{1,0:T(8,128)(2,1)} %get-tuple-element.10.x_own) | copy-start | bytes 786436
  7.5 14.1 %collective-permute-start.2 = (bf16[128,1024]{1,0:T(8,128)(2,1)}, bf16[128,1024]{1,0:T(8,128)(2,1)S(1)}, u32[]{:S(2)}, u32[]{:S(2)}) collective-permute-start(bf16[128,1024]{1,0:T(8,128)(2,1)} %get-tuple-element.13), channel_id=1, source_target_pairs={{0,12},{1,13},{2,14},{3,15},{4,0},{5,1},{6,2},{7,3},{8,4},{9,5},{1... | collective-permute-start | bytes 786440 | tf_op jit(solution)/shard_map/ppermute | solution.py:454
  21.6 1.2 %copy-start.1 = (bf16[2,2,128,1024]{3,2,1,0:T(8,128)(2,1)S(1)}, bf16[2,2,128,1024]{3,2,1,0:T(8,128)(2,1)}, u32[]{:S(2)}) copy-start(bf16[2,2,128,1024]{3,2,1,0:T(8,128)(2,1)} %get-tuple-element.9.kvt) | copy-start | bytes 3145732

commit v4 on v3

--- a/solution.py
+++ b/solution.py
@@ -433,17 +433,19 @@
 
 def deal_kernel(x_in, *outs):
     x = lax.axis_index("tp") // 4
-    wide = outs[0].shape[1] // 4
+    wide = outs[0].shape[1]
     for j in range(4):
-        for i in range(4):
-            cols = pl.ds(pl.multiple_of((4 * i + lax.rem(x + j, 4)) * wide, wide), wide)
-            outs[j][:, i * wide:(i + 1) * wide] = x_in[:, cols]
+        outs[j][...] = x_in[:, pl.ds(pl.multiple_of(lax.rem(x + j, 4) * wide, wide), wide)]
 
 
 def deal(rows):
-    vmem = pl.BlockSpec(memory_space=pltpu.VMEM)
-    shape = jax.ShapeDtypeStruct((rows.shape[0], rows.shape[1] // 4), BF16)
-    return pl.pallas_call(deal_kernel, out_shape=[shape] * 4, in_specs=[vmem], out_specs=[vmem] * 4, name="deal")(rows)
+    high, cols = rows.shape[0], rows.shape[1] // 4
+    shape = jax.ShapeDtypeStruct((high, cols), BF16)
+    return pl.pallas_call(
+        deal_kernel, out_shape=[shape] * 4, grid=(4,), name="deal",
+        in_specs=[pl.BlockSpec((high, cols), lambda i: (0, i))],
+        out_specs=[pl.BlockSpec((high, cols // 4), lambda i: (0, i))] * 4,
+    )(rows)
 
 
 def local(input_rows, queries, key_values, out_grad, item_logratio, pair_ids, tile_item, tile_image):

time: 69.5 us -> 70 us (level)
    pallas_call x1, Pallas kernels: 46.5 us -> 44.8 us  [exchange(): pl.pallas_call(exchange_kernel, out_shape=jax.ShapeDtypeStruct((PARTS * r...]
    pallas_call x1, Pallas kernels: 2.41 us -> 3.49 us  [deal(): pl.pallas_call(deal_kernel, out_shape=[shape] * 4, grid=(4,), name='deal'...]
  transfers between devices with their start and end apart: 3 -> 3, of which waited for: 0 -> 0; matrix products, arithmetic and copies ran while one was open for 0% -> 0% of each run, Pallas kernels for 18% -> 19%
where the time goes in v4:
time: 70 us; the launch traced here: 69.8 us
  Pallas kernels  61.6 us (88%)
  starting transfers between devices  5.64 us (8%)
  local copies, waits for them, and re-layouts  1.85 us (3%)
    pallas_call x1, Pallas kernels, exchange(): pl.pallas_call(exchange_kernel, out_shape=jax.ShapeDtypeStruct((PARTS * r...  44.8 us
    pallas_call x1, Pallas kernels, attention(): pl.pallas_call(attention_kernel, out_shape=[jax.ShapeDtypeStruct(queries....  13.3 us
    ppermute x3, starting transfers between devices, local(): lax.ppermute(block, 'tp', [(a, (a + 4 * dx) % 16) for a in range(16)])  5.64 us
    pallas_call x1, Pallas kernels, deal(): pl.pallas_call(deal_kernel, out_shape=[shape] * 4, grid=(4,), name='deal'...  3.49 us
    unnamed x5, local copies, waits for them, and re-layouts  1.85 us
  transfers between devices with their start and end apart: 3, of which 0 were waited for; matrix products, arithmetic and copies ran while one was open for 0% of the time, Pallas kernels for 19%

profile of v4, /device:TPU:1, one launch (start us, length us, event | category | flops | bytes accessed | tf_op | source)
XLA Modules:
  0.0 69.8 jit_solution(7831264659809036430)
XLA Ops:
  0.6 3.5 %deal.1 = (bf16[128,1024]{1,0:T(8,128)(2,1)}, bf16[128,1024]{1,0:T(8,128)(2,1)}, bf16[128,1024]{1,0:T(8,128)(2,1)}, bf16[128,1024]{1,0:T(8,128)(2,1)}) custom-call(bf16[128,4096]{1,0:T(8,128)(2,1)} %bitcast.3), custom_call_target="tpu_custom_call" | custom-call | tf_op jit(solution)/shard_map/deal/pallas_call | solution.py:444
  4.1 2.0 %collective-permute-start = (bf16[128,1024]{1,0:T(8,128)(2,1)}, bf16[128,1024]{1,0:T(8,128)(2,1)S(1)}, u32[]{:S(2)}, u32[]{:S(2)}) collective-permute-start(bf16[128,1024]{1,0:T(8,128)(2,1)} %get-tuple-element.11), channel_id=1, source_target_pairs={{0,4},{1,5},{2,6},{3,7},{4,8},{5,9},{6,10},{7,11},{8,12},{9,13},{1... | collective-permute-start | bytes 786440 | tf_op jit(solution)/shard_map/ppermute | solution.py:456
  6.2 2.5 %collective-permute-start.1 = (bf16[128,1024]{1,0:T(8,128)(2,1)}, bf16[128,1024]{1,0:T(8,128)(2,1)S(1)}, u32[]{:S(2)}, u32[]{:S(2)}) collective-permute-start(bf16[128,1024]{1,0:T(8,128)(2,1)} %get-tuple-element.12), channel_id=1, source_target_pairs={{0,8},{1,9},{2,10},{3,11},{4,12},{5,13},{6,14},{7,15},{8,0},{9,1},... | collective-permute-start | bytes 786440 | tf_op jit(solution)/shard_map/ppermute | solution.py:456
  8.6 0.0 copy-start
  8.6 1.2 %collective-permute-start.2 = (bf16[128,1024]{1,0:T(8,128)(2,1)}, bf16[128,1024]{1,0:T(8,128)(2,1)S(1)}, u32[]{:S(2)}, u32[]{:S(2)}) collective-permute-start(bf16[128,1024]{1,0:T(8,128)(2,1)} %get-tuple-element.13), channel_id=1, source_target_pairs={{0,12},{1,13},{2,14},{3,15},{4,0},{5,1},{6,2},{7,3},{8,4},{9,5},{1... | collective-permute-start | bytes 786440 | tf_op jit(solution)/shard_map/ppermute | solution.py:456
  9.8 13.3 %attention.1 = (bf16[1,2048,256]{2,1,0:T(8,128)(2,1)}, bf16[2,2,128,1024]{3,2,1,0:T(8,128)(2,1)}) custom-call(f32[1,4]{1,0:T(1,128)} %ratio_h.1, s32[1,4]{1,0:T(1,128)} %pair_h.1, s32[1,16]{1,0:T(1,128)} %item_h.1, s32[1,16]{1,0:T(1,128)} %image_h.1, bf16[1,2048,256]{2,1,0:T(8,128)(2,1)} %q_hbm.1, bf16[1,2048,256]{2,1,0:T(8,128)(2,1)} %og_hbm.1, ...), custom_call_target="tpu_custom_call" | custom-call | flops 10000000000 | bytes 8388608 | tf_op jit(solution)/shard_map/attention/pallas_call | solution.py:204
  23.1 0.0 collective-permute-done.x1
  23.1 0.0 collective-permute-done.1.x2
  23.1 0.0 collective-permute-done.2.x3
  23.1 0.0 copy-done
  23.1 0.0 copy-start.1
  23.1 1.2 %copy-done.1 = bf16[2,2,128,1024]{3,2,1,0:T(8,128)(2,1)S(1)} copy-done((bf16[2,2,128,1024]{3,2,1,0:T(8,128)(2,1)S(1)}, bf16[2,2,128,1024]{3,2,1,0:T(8,128)(2,1)}, u32[]{:S(2)}) %copy-start.1) | copy-done | bytes 1048600
  24.4 44.8 %exchange.1 = f32[64,256]{1,0:T(8,128)S(1)} custom-call(bf16[2,2,128,1024]{3,2,1,0:T(8,128)(2,1)S(1)} %copy-done.1, bf16[128,1024]{1,0:T(8,128)(2,1)S(1)} %copy-done, bf16[128,1024]{1,0:T(8,128)(2,1)S(1)} %collective-permute-done.x1, bf16[128,1024]{1,0:T(8,128)(2,1)S(1)} %collective-permute-done.1.x2, bf16[128,1024]{1,0:T(8,128)(2,1)S(1)} %collective-permute-done.2.x3), custom_call_target="tpu_custom_call" | custom-call | flops 1000000000 | bytes 8388608 | tf_op jit(solution)/shard_map/exchange/pallas_call | solution.py:413
  69.2 0.6 copy.11
Async XLA Ops:
  4.1 19.0 %collective-permute-start = (bf16[128,1024]{1,0:T(8,128)(2,1)}, bf16[128,1024]{1,0:T(8,128)(2,1)S(1)}, u32[]{:S(2)}, u32[]{:S(2)}) collective-permute-start(bf16[128,1024]{1,0:T(8,128)(2,1)} %get-tuple-element.11), channel_id=1, source_target_pairs={{0,4},{1,5},{2,6},{3,7},{4,8},{5,9},{6,10},{7,11},{8,12},{9,13},{1... | collective-permute-start | bytes 786440 | tf_op jit(solution)/shard_map/ppermute | solution.py:456
  6.2 16.9 %collective-permute-start.1 = (bf16[128,1024]{1,0:T(8,128)(2,1)}, bf16[128,1024]{1,0:T(8,128)(2,1)S(1)}, u32[]{:S(2)}, u32[]{:S(2)}) collective-permute-start(bf16[128,1024]{1,0:T(8,128)(2,1)} %get-tuple-element.12), channel_id=1, source_target_pairs={{0,8},{1,9},{2,10},{3,11},{4,12},{5,13},{6,14},{7,15},{8,0},{9,1},... | collective-permute-start | bytes 786440 | tf_op jit(solution)/shard_map/ppermute | solution.py:456
  8.6 14.5 %copy-start = (bf16[128,1024]{1,0:T(8,128)(2,1)S(1)}, bf16[128,1024]{1,0:T(8,128)(2,1)}, u32[]{:S(2)}) copy-start(bf16[128,1024]{1,0:T(8,128)(2,1)} %get-tuple-element.10.x_own) | copy-start | bytes 786436
  8.6 14.5 %collective-permute-start.2 = (bf16[128,1024]{1,0:T(8,128)(2,1)}, bf16[128,1024]{1,0:T(8,128)(2,1)S(1)}, u32[]{:S(2)}, u32[]{:S(2)}) collective-permute-start(bf16[128,1024]{1,0:T(8,128)(2,1)} %get-tuple-element.13), channel_id=1, source_target_pairs={{0,12},{1,13},{2,14},{3,15},{4,0},{5,1},{6,2},{7,3},{8,4},{9,5},{1... | collective-permute-start | bytes 786440 | tf_op jit(solution)/shard_map/ppermute | solution.py:456
  23.1 1.2 %copy-start.1 = (bf16[2,2,128,1024]{3,2,1,0:T(8,128)(2,1)S(1)}, bf16[2,2,128,1024]{3,2,1,0:T(8,128)(2,1)}, u32[]{:S(2)}) copy-start(bf16[2,2,128,1024]{3,2,1,0:T(8,128)(2,1)} %get-tuple-element.9.kvt) | copy-start | bytes 3145732
